TPU v7x, 256 devices: a whole 4x4x8 slice. The times are simulated.
256 devices in a mesh: ep: 8 (over z_hi, x), fsdp: 32 (over y, z_lo, core).
Axes of the slice: x: 4, y: 4, z: 8 (z_hi: 2, z_lo: 4; z = z_hi * 4 + z_lo), core: 2. Of those that a mesh axis runs over, the one named last changes fastest.
Arguments:
- tokens: bfloat16 [1024, 6144], P('ep', 'fsdp'), may hold values from -6 to 6
- expert_ids: int32 [1024, 2], P('ep'), may hold values from 0 to 7, all different within a row; in each aligned block of 128 rows (0 to 127, 128 to 255, ...) at most 64 rows name the same one
- combine_weights: float32 [1024, 2], P('ep'), may hold values from 0.25 to 1
- w_gate: bfloat16 [8, 6144, 8192], P('ep', None, 'fsdp'), may hold values from -0.078125 to 0.078125
- w_up: bfloat16 [8, 6144, 8192], P('ep', None, 'fsdp'), may hold values from -0.078125 to 0.078125
- w_down: bfloat16 [8, 8192, 6144], P('ep', 'fsdp'), may hold values from -0.0625 to 0.0625
Outputs:
- mixed_rows: bfloat16 [1024, 6144], P('ep', 'fsdp')
Inputs may be any that keep to these rules, and one draw needn't show every extreme that they name: `expert_ids`: among the 128 tokens of one index of ep (aligned blocks of rows), no expert is named by more than 64 rows, a bound that some block reaches; a token names two different experts.
All inputs are finite; a program needn't handle non-finite values.
Results may differ from a plain program's by a relative error of at most 0.0057.
Values may be sent and summed in bfloat16 or wider, within the bound.
No kernel may reach another device: no remote copies, remote signals or barrier semaphores. Data moves between devices by JAX's collectives and lax.ppermute only.
A program may use at most 128 MiB of HBM per device.

v0:
```python
import jax
import jax.numpy as jnp
from jax import lax
from jax.sharding import PartitionSpec as P


def shards(tokens, expert_ids, combine_weights, w_gate, w_up, w_down):
    groups = lax.axis_size("ep")
    tok_rows = tokens.shape[0]
    width_local = tokens.shape[1]
    capacity = min(tok_rows, 4 * tok_rows // groups)
    experts_all = groups * w_gate.shape[0]
    chosen = expert_ids.reshape(-1)
    expert_lane = jnp.arange(experts_all, dtype=jnp.int32)
    onehot = (chosen[:, None] == expert_lane[None, :]).astype(jnp.int32)
    before = jnp.cumsum(onehot, axis=0, dtype=jnp.int32) - onehot
    slot_index = jnp.sum(before * onehot, axis=1)
    position = (chosen * capacity + slot_index).reshape(tok_rows, 2)
    places = jnp.arange(experts_all * capacity, dtype=jnp.int32)
    select = position[:, :, None] == places[None, None, :]
    dispatch = jnp.sum(select.astype(jnp.float32), axis=1).astype(jnp.bfloat16)
    packed = lax.dot_general(
        dispatch, tokens, (((0,), (0,)), ((), ())), preferred_element_type=jnp.float32
    )
    packed = packed.astype(jnp.bfloat16).reshape(experts_all, capacity, width_local)
    arrived = lax.all_to_all(packed, "ep", split_axis=0, concat_axis=0, tiled=True)
    expert_rows = arrived.reshape(groups * capacity, width_local)
    gate_local = w_gate[0]
    up_local = w_up[0]
    down_local = w_down[0]
    section = lax.all_gather(expert_rows, "fsdp", axis=1, tiled=True)
    gate_sums = jnp.dot(section, gate_local, preferred_element_type=jnp.float32)
    up_sums = jnp.dot(section, up_local, preferred_element_type=jnp.float32)
    hidden = (jax.nn.silu(gate_sums) * up_sums).astype(jnp.bfloat16)
    summed = lax.psum_scatter(
        lax.dot_general(
            down_local, hidden, (((0,), (1,)), ((), ())), preferred_element_type=jnp.float32
        ),
        "fsdp",
        scatter_dimension=0,
        tiled=True,
    )
    result = summed.T.astype(jnp.bfloat16)
    returned = lax.all_to_all(
        result.reshape(groups, capacity, width_local), "ep", split_axis=0, concat_axis=0, tiled=True
    )
    weighting = jnp.sum(jnp.where(select, combine_weights[:, :, None], 0.0), axis=1)
    mixed_rows = jnp.dot(
        weighting,
        returned.reshape(-1, width_local).astype(jnp.float32),
        precision=lax.Precision.HIGHEST,
    )
    return mixed_rows.astype(jnp.bfloat16)


def solution(mesh):
    in_specs = (
        P("ep", "fsdp"),
        P("ep", None),
        P("ep", None),
        P("ep", None, "fsdp"),
        P("ep", None, "fsdp"),
        P("ep", "fsdp", None),
    )
    out_specs = P("ep", "fsdp")
    return jax.shard_map(shards, mesh=mesh, in_specs=in_specs, out_specs=out_specs, check_vma=False)
```

profile of v0, /device:TPU:2, one launch (start us, length us, event | category | flops | bytes accessed | tf_op | source)
XLA Modules:
  0.0 336.2 jit_solution(7917061776976984634)
XLA Ops:
  6.5 0.9 copy.29
  7.5 0.1 eq.42
  7.6 0.1 eq.38
  7.8 0.6 reduce-window.6
  8.4 0.2 slice_reduce_fusion
  8.6 0.1 fusion.21
  8.7 0.1 reduce_sum.30
  8.9 0.1 copy.31
  8.9 0.7 multiply_add_fusion
  9.6 1.6 convert_reduce_fusion
  11.2 1.7 convolution_convert_fusion
  12.8 1.1 copy.32
  13.9 20.8 %all_to_all.10 = bf16[8,64,192]{2,1,0:T(8,128)(2,1)} all-to-all(bf16[8,64,192]{2,1,0:T(8,128)(2,1)S(1)} %bitcast.38), channel_id=1, replica_groups=mesh['ep'=8,'fsdp'=32] {'ep'}, dimensions={0} | all-to-all | bytes 393216 | tf_op jit(solution)/shard_map/all_to_all | solution.py:26
  34.7 1.8 copy.33
  36.5 0.0 all-gather.2.cloned.1.call-update
  36.5 0.0 reduce-scatter.4.cloned.1.call-start
  36.5 65.6 %all-gather.2.cloned.1.call-done = bf16[512,6144]{0,1:T(8,128)(2,1)} async-done(((bf16[512,192]{0,1:T(8,128)(2,1)}), bf16[512,6144]{0,1:T(8,128)(2,1)}) %all-gather.2.cloned.1.call-update) | async-done | bytes 6291472 | tf_op jit(solution)/shard_map/all_gather | solution.py:31
  102.2 6.3 %fusion.3 = f32[512,256]{1,0:T(8,128)} fusion(bf16[512,6144]{0,1:T(8,128)(2,1)} %all-gather.2.cloned.1.call-done, bf16[1,6144,256]{2,1,0:T(8,128)(2,1)} %param.9), kind=kOutput, calls=%fused_computation.4 | convolution fusion | flops 1610612736 | bytes 9961472 | tf_op jit(solution)/shard_map/dot_general | solution.py:32
  108.5 15.0 %convolution_bitcast_fusion = f32[6144,512]{0,1:T(8,128)} fusion(bf16[1,256,6144]{2,1,0:T(8,128)(2,1)S(1)} %copy-done, bf16[512,6144]{0,1:T(8,128)(2,1)} %all-gather.2.cloned.1.call-done, bf16[1,6144,256]{2,1,0:T(8,128)(2,1)} %param.10, f32[512,256]{1,0:T(8,128)} %fusion.3), kind=kOutput, calls=%fused_computation | convolution fusion | flops 3222011904 | bytes 25690112 | tf_op jit(solution)/shard_map/dot_general | solution.py:36
  123.5 12.6 %copy.34 = f32[6144,512]{1,0:T(8,128)} copy(f32[6144,512]{0,1:T(8,128)} %convolution_bitcast_fusion) | data formatting | bytes 25165824
  136.1 174.5 %reduce-scatter.4.cloned.1.call-done = f32[192,512]{1,0:T(8,128)} async-done(((f32[6144,512]{1,0:T(8,128)}), f32[192,512]{1,0:T(8,128)}) %reduce-scatter.4.cloned.1.call-update) | async-done | bytes 393232
  310.6 1.8 copy.35
  312.4 15.9 %all_to_all.11 = bf16[8,64,192]{2,1,0:T(8,128)(2,1)S(1)} all-to-all(bf16[8,64,192]{2,1,0:T(8,128)(2,1)} %bitcast.41), channel_id=1, replica_groups=mesh['ep'=8,'fsdp'=32] {'ep'}, dimensions={0} | all-to-all | bytes 393216 | tf_op jit(solution)/shard_map/all_to_all | solution.py:44
  328.4 1.0 convolution_convert_fusion.1
  (9 shorter events, 0.1 us)
Async XLA Ops:
  6.5 102.0 %copy-start = (bf16[1,256,6144]{2,1,0:T(8,128)(2,1)S(1)}, bf16[1,256,6144]{2,1,0:T(8,128)(2,1)}, u32[]{:S(2)}) copy-start(bf16[1,256,6144]{2,1,0:T(8,128)(2,1)} %param.11) | copy-start | bytes 9437188
  6.5 95.6 %all-gather.2.cloned.1.call-start = ((), (), s32[]{:S(2)}) async-start(), calls=%async_computation.3 | async-start | bytes 6488064 | tf_op jit(solution)/shard_map/all_gather | solution.py:31
  36.5 274.1 %reduce-scatter.4.cloned.1.call-start = ((), (), s32[]{:S(2)}) async-start(), calls=%async_computation.4 | async-start | bytes 12976128
  136.1 192.3 %copy-start.1 = (f32[128,512]{1,0:T(8,128)S(1)}, f32[128,512]{1,0:T(8,128)}, u32[]{:S(2)}) copy-start(f32[128,512]{1,0:T(8,128)} %get-tuple-element.6) | copy-start | bytes 786436
Sparse Core Ops, SparseCore 0:
  36.6 65.5 all-gather.1
  136.3 174.3 reduce-scatter.3
where the time goes:
time: 337 us; the launch traced here: 336 us
  waiting for transfers between devices  240 us (71%)
  blocking collectives  36.7 us (11%)
  matrix products  24 us (7%)
  local copies, waits for them, and re-layouts  18.9 us (6%)
  between operations  13.4 us (4%)
    unnamed x3, waiting for transfers between devices  175 us
    all_gather x1, waiting for transfers between devices, shards(): section = lax.all_gather(expert_rows, 'fsdp', axis=1, tiled=True)  65.6 us
    all_to_all x1, blocking collectives, shards(): lax.all_to_all(packed, 'ep', split_axis=0, concat_axis=0, tiled=True)  20.8 us
    all_to_all x1, blocking collectives, shards(): lax.all_to_all(result.reshape(groups, capacity, width_local), 'ep', split...  15.9 us
    unnamed x7, local copies, waits for them, and re-layouts  15.4 us
    dot_general x1, matrix products, shards(): lax.dot_general(down_local, hidden, (((0,), (1,)), ((), ())), preferred_e...  15 us
  transfers between devices with their start and end apart: 2, of which 2 were waited for; matrix products, arithmetic and copies ran while one was open for 0% of the time, Pallas kernels for 0%

commit v1 on v0

--- a/solution.py
+++ b/solution.py
@@ -2,6 +2,11 @@
 import jax.numpy as jnp
 from jax import lax
 from jax.sharding import PartitionSpec as P
+
+
+def swapped_in(shard, axis, along):
+    stack = jnp.stack([shard] * lax.axis_size(axis))
+    return jnp.concatenate(lax.all_to_all(stack, axis, 0, 0), axis=along)
 
 
 def shards(tokens, expert_ids, combine_weights, w_gate, w_up, w_down):
@@ -28,7 +33,7 @@
     gate_local = w_gate[0]
     up_local = w_up[0]
     down_local = w_down[0]
-    section = lax.all_gather(expert_rows, "fsdp", axis=1, tiled=True)
+    section = swapped_in(expert_rows, "fsdp", 1)
     gate_sums = jnp.dot(section, gate_local, preferred_element_type=jnp.float32)
     up_sums = jnp.dot(section, up_local, preferred_element_type=jnp.float32)
     hidden = (jax.nn.silu(gate_sums) * up_sums).astype(jnp.bfloat16)

time: 337 us -> 414 us (1.23)
  blocking collectives: 36.7 us -> 187 us
  waiting for transfers between devices: 240 us -> 168 us
    all_to_all x0 -> x1, blocking collectives: none -> 149 us  [swapped_in(): return jnp.concatenate(lax.all_to_all(stack, axis, 0, 0), axis=along)]
    all_gather x1 -> x0, waiting for transfers between devices: 65.6 us -> none  [shards(): section = lax.all_gather(expert_rows, 'fsdp', axis=1, tiled=True)]
    unnamed x3 -> x2, waiting for transfers between devices: 175 us -> 168 us
    unnamed x7 -> x11, local copies, waits for them, and re-layouts: 15.4 us -> 18 us
  transfers between devices with their start and end apart: 2 -> 1, of which waited for: 2 -> 1; matrix products, arithmetic and copies ran while one was open for 0% -> 0% of each run, Pallas kernels for 0% -> 0%
where the time goes in v1:
time: 414 us
  blocking collectives  187 us (45%)
  waiting for transfers between devices  168 us (41%)
  local copies, waits for them, and re-layouts  21.5 us (5%)
  matrix products  20.3 us (5%)
  between operations  13.5 us (3%)
    unnamed x2, waiting for transfers between devices  168 us
    all_to_all x1, blocking collectives, swapped_in(): return jnp.concatenate(lax.all_to_all(stack, axis, 0, 0), axis=along)  149 us
    all_to_all x1, blocking collectives, shards(): lax.all_to_all(packed, 'ep', split_axis=0, concat_axis=0, tiled=True)  20.8 us
    unnamed x11, local copies, waits for them, and re-layouts  18 us
    all_to_all x1, blocking collectives, shards(): lax.all_to_all(result.reshape(groups, capacity, width_local), 'ep', split...  17.2 us
    dot_general x1, matrix products, shards(): lax.dot_general(down_local, hidden, (((0,), (1,)), ((), ())), preferred_e...  15 us
  transfers between devices with their start and end apart: 1, of which 1 were waited for; matrix products, arithmetic and copies ran while one was open for 0% of the time, Pallas kernels for 0%

profile of v1, /device:TPU:2, one launch (start us, length us, event | category | flops | bytes accessed | tf_op | source)
XLA Modules:
  0.0 413.6 jit_solution(5786549004810088262)
XLA Ops:
  6.5 0.9 copy.31
  7.5 0.1 eq.42
  7.6 0.1 eq.38
  7.8 0.6 reduce-window.6
  8.4 0.2 slice_reduce_fusion
  8.6 0.1 fusion.21
  8.7 0.1 reduce_sum.30
  8.9 0.1 copy.33
  8.9 0.7 multiply_add_fusion
  9.6 1.6 convert_reduce_fusion
  11.2 1.7 convolution_convert_fusion
  12.8 1.1 copy.34
  13.9 20.8 %all_to_all.15 = bf16[8,64,192]{2,1,0:T(8,128)(2,1)} all-to-all(bf16[8,64,192]{2,1,0:T(8,128)(2,1)S(1)} %bitcast.43), channel_id=1, replica_groups=mesh['ep'=8,'fsdp'=32] {'ep'}, dimensions={0} | all-to-all | bytes 393216 | tf_op jit(solution)/shard_map/all_to_all | solution.py:31
  34.7 1.1 copy.35
  35.8 0.7 stack.3
  36.5 148.8 %all_to_all.16 = bf16[32,512,192]{1,2,0:T(8,128)(2,1)S(1)} all-to-all(bf16[32,512,192]{1,2,0:T(8,128)(2,1)S(1)} %stack.3), channel_id=1, replica_groups=mesh['ep'=8,'fsdp'=32] {'fsdp'}, dimensions={0} | all-to-all | bytes 12582912 | tf_op jit(solution)/shard_map/all_to_all | solution.py:9
  185.3 2.6 copy-done.1
  188.0 2.6 fusion.3
  190.6 15.0 %convolution_bitcast_fusion = f32[6144,512]{0,1:T(8,128)} fusion(bf16[1,256,6144]{2,1,0:T(8,128)(2,1)S(1)} %copy-done, bf16[512,6144]{0,1:T(8,128)(2,1)} %bitcast.42, bf16[1,6144,256]{2,1,0:T(8,128)(2,1)} %param.10, f32[512,256]{1,0:T(8,128)} %fusion.3), kind=kOutput, calls=%fused_computation | convolution fusion | flops 3222011904 | bytes 25690112 | tf_op jit(solution)/shard_map/dot_general | solution.py:41
  205.6 12.6 %copy.36 = f32[6144,512]{1,0:T(8,128)} copy(f32[6144,512]{0,1:T(8,128)} %convolution_bitcast_fusion) | data formatting | bytes 25165824
  218.2 168.5 %reduce-scatter.4.cloned.1.call-done = f32[192,512]{1,0:T(8,128)} async-done(((f32[6144,512]{1,0:T(8,128)}), f32[192,512]{1,0:T(8,128)}) %reduce-scatter.4.cloned.1.call-update) | async-done | bytes 393232
  386.7 1.8 copy.37
  388.5 17.2 %all_to_all.17 = bf16[8,64,192]{2,1,0:T(8,128)(2,1)S(1)} all-to-all(bf16[8,64,192]{2,1,0:T(8,128)(2,1)} %bitcast.46), channel_id=1, replica_groups=mesh['ep'=8,'fsdp'=32] {'ep'}, dimensions={0} | all-to-all | bytes 393216 | tf_op jit(solution)/shard_map/all_to_all | solution.py:49
  405.7 1.0 convolution_convert_fusion.1
  (12 shorter events, 0.1 us)
Async XLA Ops:
  6.5 184.0 %copy-start = (bf16[1,256,6144]{2,1,0:T(8,128)(2,1)S(1)}, bf16[1,256,6144]{2,1,0:T(8,128)(2,1)}, u32[]{:S(2)}) copy-start(bf16[1,256,6144]{2,1,0:T(8,128)(2,1)} %param.11) | copy-start | bytes 9437188
  6.5 380.2 %reduce-scatter.4.cloned.1.call-start = ((), (), s32[]{:S(2)}) async-start(), calls=%async_computation.4 | async-start | bytes 12976128
  36.5 151.5 %copy-start.2 = (bf16[1,6144,256]{2,1,0:T(8,128)(2,1)S(1)}, bf16[1,6144,256]{2,1,0:T(8,128)(2,1)}, u32[]{:S(2)}) copy-start(bf16[1,6144,256]{2,1,0:T(8,128)(2,1)} %param.9) | copy-start | bytes 9437188
  185.3 2.6 copy-start.1
  218.2 187.5 %copy-start.3 = (f32[128,512]{1,0:T(8,128)S(1)}, f32[128,512]{1,0:T(8,128)}, u32[]{:S(2)}) copy-start(f32[128,512]{1,0:T(8,128)} %get-tuple-element.6) | copy-start | bytes 786436
Sparse Core Ops, SparseCore 0:
  218.3 168.3 reduce-scatter.3
